TPU v7x, 256 devices: a whole 4x4x8 slice. The times are simulated.
256 devices in a mesh: dp: 8 (over x, core), expert: 32 (over y, z).
Axes of the slice: x: 4, y: 4, z: 8, core: 2. Of those that a mesh axis runs over, the one named last changes fastest.
Arguments:
- tokens: bfloat16 [32768, 3072], P(('dp', 'expert')), may hold values from -24 to 24
- norm_gain: float32 [3072], replicated, may hold values from 0.1 to 1.9
- experts_chosen: int32 [32768, 4], P(('dp', 'expert')), may hold values from 0 to 31, all different within a row; in each aligned block of 128 rows (0 to 127, 128 to 255, ...) at most 18 rows name the same one
- gate_weights: float32 [32768, 4], P(('dp', 'expert')), may hold values from 0.1 to 0.6
- expert_up: bfloat16 [32, 3072, 768], P('expert'), may hold values from -0.109375 to 0.109375
- expert_down: bfloat16 [32, 768, 3072], P('expert'), may hold values from -0.21875 to 0.21875
- head_cond: bfloat16 [3072, 768], P(('dp', 'expert')), may hold values from -0.109375 to 0.109375
- head_in: bfloat16 [16, 768], replicated, may hold values from -1.5 to 1.5
- head_gain: float32 [768], replicated, may hold values from 0.1 to 1.9
- head_out: bfloat16 [16, 768], replicated, may hold values from -0.21875 to 0.21875
- latents: float32 [16, 32768], P(None, ('dp', 'expert')), may hold values from -6 to 6
- noise_draws: float32 [4, 16, 32768], P(None, None, ('dp', 'expert')), may hold values from -6 to 6
- timesteps: int32 [4, 32768], P(None, ('dp', 'expert')), may hold values from 0 to 999
Outputs:
- input_grad: bfloat16 [32768, 3072], P(('dp', 'expert'))
- cond_grad: float32 [3072, 768], P(('dp', 'expert'))
- entry_grad: float32 [16, 768], replicated
- exit_grad: float32 [16, 768], replicated
- gain_grad: float32 [768], replicated
- mean_loss: float32 [], replicated
Inputs may be any that keep to these rules, and one draw needn't show every extreme that they name: `experts_chosen`: each row names 4 different experts; among the rows of one device no expert is named by more than 18 rows, a bound that some block reaches.
All inputs are finite; a program needn't handle non-finite values.
Results may differ from a plain program's by a relative error of at most 0.0095.
Values may be sent and summed in bfloat16 or wider, within the bound.
No kernel may reach another device: no remote copies, remote signals or barrier semaphores. Data moves between devices by JAX's collectives and lax.ppermute only.
A program may use at most 128 MiB of HBM per device.

v0:
```python
import math

import jax
import jax.numpy as jnp
from jax import lax
from jax.experimental import pallas as pl
from jax.experimental.pallas import tpu as pltpu
from jax.sharding import Mesh, PartitionSpec as P

HW = 768
TOPK = 4
NOISE = 4
TSTEPS = 1000


NORM_EPS = 1e-06
ROOT_COEF = math.sqrt(2.0 / math.pi)
HIGH = lax.Precision.HIGHEST
DP = ("x", "core")
EXPERT = ("y", "z")
EVERY = DP + EXPERT
CORES = 2
RING = 8
F32 = jnp.float32
BF16 = jnp.bfloat16

MAIN = 16
REST = 8
WIDE = 4
LESS_PART = 256
MORE_PART = 512
HALF_PART = 384
TAIL = 40
NARROW = 3
NARROW_PART = 256
LANES = 128
ENTRY_ROW = 0
EXIT_ROW = 96
GAIN_ROW = 192
LOSS_ROW = 198


def gelu_tanh(values):
    inner = ROOT_COEF * (values + 0.044715 * values * values * values)
    return 0.5 * values * (1.0 + jnp.tanh(inner))


def gelu_slope(values):
    inner = ROOT_COEF * (values + 0.044715 * values * values * values)
    tangent = jnp.tanh(inner)
    return 0.5 * (1.0 + tangent) + 0.5 * values * (1.0 - tangent * tangent) * ROOT_COEF * (
        1.0 + 3.0 * 0.044715 * values * values
    )


def signal_level(step_ids):
    fraction = (step_ids.astype(jnp.float32) / TSTEPS + 0.008) / 1.008
    cosine = jnp.cos(fraction * (math.pi / 2.0))
    return cosine * cosine


def time_embed(step_ids):
    half_width = HW // 2
    frequency = jnp.exp(-math.log(10000.0) * jnp.arange(half_width, dtype=jnp.float32) / half_width)
    angles = step_ids.astype(jnp.float32)[:, None] * frequency[None, :]
    return jnp.concatenate([jnp.cos(angles), jnp.sin(angles)], axis=1)


def matmul(left, right, left_dim=1, right_dim=0, precision=None):
    return lax.dot_general(
        left, right, (((left_dim,), (right_dim,)), ((), ())),
        precision=precision, preferred_element_type=F32,
    )


def iota(shape, axis):
    return lax.broadcasted_iota(jnp.int32, shape, axis)


def of_part(rows, part):
    return ((iota((rows, 1), 0) & 7) >> 1) == part


def rest_rows(peers, part):
    row, col = iota((peers * 2, peers * REST), 0), iota((peers * 2, peers * REST), 1)
    return jnp.where(col == (row >> 1) * REST + part * 2 + (row & 1), 1.0, 0.0).astype(BF16)


def rest_spread(peers, part):
    row, col = iota((peers * REST, peers * 2), 0), iota((peers * REST, peers * 2), 1)
    return jnp.where(row == (col >> 1) * REST + part * 2 + (col & 1), 1.0, 0.0).astype(BF16)


def bring(sources, targets, sems):
    copies = [pltpu.make_async_copy(*ends, sems.at[i]) for i, ends in enumerate(zip(sources, targets))]
    for copy in copies:
        copy.start()
    return copies


def flat(block):
    return block.reshape(block.shape[0] * block.shape[1], block.shape[2])


def main_of(block, part):
    return flat(block[:, MAIN * part : MAIN * (part + 1), :])


def rest_of(block, parts):
    return flat(block[:, MAIN * parts : MAIN * parts + REST, :].astype(F32)).astype(BF16)


def dispatch_kernel(
    tokens_in, gain_in, chosen_in, gates_in, cond_in, send_ref, later_ref, gate_ref, inverse_ref,
    normed_ref, tokens_ref, gain_ref, chosen_ref, gates_ref, cond_ref, own_ref, sems,
):
    step = pl.program_id(0)
    tok_rows = tokens_ref.shape[0]
    experts = gate_ref.shape[0] // (MAIN + REST)
    group = send_ref.shape[0]
    main_rows = experts * MAIN

    @pl.when(step == 0)
    def _():
        sources = (tokens_in, gain_in, chosen_in, gates_in, cond_in)
        for copy in bring(sources, (tokens_ref, gain_ref, chosen_ref, gates_ref, cond_ref), sems):
            copy.wait()
        own_ref[...] = jnp.zeros_like(own_ref)
        cond = cond_ref[...].astype(F32)
        cond_rows = cond.shape[0]
        for piece in range(NARROW):
            columns = slice(piece * NARROW_PART, (piece + 1) * NARROW_PART)
            own_ref[piece * cond_rows : (piece + 1) * cond_rows, :] = cond[:, columns]
        inputs = tokens_ref[...].astype(F32)
        inverse = lax.rsqrt(jnp.mean(inputs * inputs, axis=1, keepdims=True) + NORM_EPS)
        inverse_ref[...] = inverse
        normed_ref[...] = (inputs * inverse * gain_ref[...]).astype(BF16)
        ids = iota((experts, tok_rows), 0)
        named = jnp.zeros((experts, tok_rows), F32)
        gate_of = jnp.zeros((experts, tok_rows), F32)
        for choice in range(TOPK):
            hit = chosen_ref[choice : choice + 1, :] == ids
            named = named + jnp.where(hit, 1.0, 0.0)
            gate_of = gate_of + jnp.where(hit, gates_ref[choice : choice + 1, :], 0.0)
        earlier = jnp.where(iota((tok_rows, tok_rows), 0) < iota((tok_rows, tok_rows), 1), 1.0, 0.0)
        named = named.astype(BF16)
        before = matmul(named, earlier.astype(BF16)).astype(BF16)

        def slots(first, rows, shift, slot):
            spread = jnp.where((iota((rows, experts), 0) >> shift) == iota((rows, experts), 1), 1.0, 0.0)
            spread_bf = spread.astype(BF16)
            held = (matmul(spread_bf, named) > 0.5) & (matmul(spread_bf, before) == slot.astype(F32))
            gates = matmul(spread, gate_of, precision=HIGH)
            gate_ref[first : first + rows, :] = jnp.where(held, gates, 0.0)

        slots(0, main_rows, 4, iota((main_rows, tok_rows), 0) & 15)
        rows = experts * REST
        slots(main_rows, rows, 3, 16 + (iota((rows, tok_rows), 0) & 1))

    main_at = pl.multiple_of(step * (group * MAIN), group * MAIN)
    rest_at = pl.multiple_of(main_rows + step * (group * REST), group * REST)
    pick = jnp.where(gate_ref[pl.ds(main_at, group * MAIN), :] != 0.0, 1.0, 0.0).astype(BF16)
    rest = jnp.where(gate_ref[pl.ds(rest_at, group * REST), :] != 0.0, 1.0, 0.0)
    first = 0
    for out_ref in (send_ref, later_ref):
        width = out_ref.shape[2]
        total = jnp.zeros((group * REST, width), F32)
        for part in range(WIDE):
            piece = normed_ref[:, first : first + width]
            first = first + width
            main = matmul(pick, piece).astype(BF16)
            out_ref[:, MAIN * part : MAIN * (part + 1), :] = main.reshape(group, MAIN, width)
            total = total + matmul(jnp.where(of_part(group * REST, part), rest, 0.0).astype(BF16), piece)
        tail = total.reshape(group, REST, width)
        if out_ref is send_ref:
            own = jnp.broadcast_to(own_ref[...][None], (group,) + own_ref.shape)
            tail = jnp.concatenate([tail, own], axis=1)
        out_ref[:, MAIN * WIDE :, :] = tail.astype(BF16)


def gather_rows(rows_ref, held_ref, part, column):
    peers = rows_ref.shape[0]
    main_rows = peers * MAIN
    main = rows_ref[:, pl.ds(pl.multiple_of(part * MAIN, MAIN), MAIN), :]
    columns = slice(column, column + rows_ref.shape[2])
    held_ref[:main_rows, columns] = flat(main)
    held_ref[main_rows:, columns] = matmul(rest_rows(peers, part), rest_of(rows_ref, WIDE)).astype(BF16)


def first_kernel(rows_ref, up_ref, pre_ref, held_ref):
    step = pl.program_id(0)
    gather_rows(rows_ref, held_ref, 2 * step, 0)
    gather_rows(rows_ref, held_ref, 2 * step + 1, rows_ref.shape[2])
    product = matmul(held_ref[...], up_ref[...])

    @pl.when(step == 0)
    def _():
        pre_ref[...] = product

    @pl.when(step > 0)
    def _():
        pre_ref[...] += product


def forward_kernel(
    rows_ref, up_ref, start_in, mixed_in, pre_ref, hidden_ref, send_ref, held_ref, start_ref, mixed_ref, sems
):
    step = pl.program_id(0)
    start_copy = pltpu.make_async_copy(start_in, start_ref, sems.at[0])
    mixed_copy = pltpu.make_async_copy(mixed_in, mixed_ref, sems.at[1])

    @pl.when(step == 0)
    def _():
        start_copy.start()
        mixed_copy.start()

    peers = rows_ref.shape[0]
    main_rows = peers * MAIN
    gather_rows(rows_ref, held_ref, 2 * step, 0)
    gather_rows(rows_ref, held_ref, 2 * step + 1, rows_ref.shape[2])
    product = matmul(held_ref[...], up_ref[...])

    @pl.when(step == 0)
    def _():
        start_copy.wait()
        pre_ref[...] = start_ref[...] + product

    @pl.when(step == WIDE // 2 - 1)
    def _():
        pre_act = pre_ref[...] + product
        pre_ref[...] = pre_act
        hidden = gelu_tanh(pre_act).astype(BF16)
        hidden_ref[...] = hidden
        mixed_copy.wait()
        added = matmul(hidden, mixed_ref[...]).astype(BF16)
        total = jnp.zeros((peers * REST, NARROW_PART), F32)
        for piece in range(NARROW):
            columns = slice(piece * NARROW_PART, (piece + 1) * NARROW_PART)
            send_ref[:, MAIN * piece : MAIN * (piece + 1), :] = added[:main_rows, columns].reshape(
                peers, MAIN, NARROW_PART
            )
            total = total + matmul(rest_spread(peers, piece), added[main_rows:, columns])
        send_ref[:, MAIN * NARROW :, :] = total.reshape(peers, REST, NARROW_PART).astype(BF16)


def two(values):
    high = values.astype(BF16).astype(F32)
    return jnp.concatenate([high, values - high], axis=values.ndim - 1)


def three(values, axis):
    high = values.astype(BF16)
    left = values - high.astype(F32)
    middle = left.astype(BF16)
    return jnp.concatenate([high, middle, (left - middle.astype(F32)).astype(BF16)], axis=axis)


def of_three(rows):
    third = rows.shape[0] // 3
    return rows[:third] + rows[third : 2 * third] + rows[2 * third :]


def head_kernel(
    added_ref, direct_ref, offset_in, noisy_ref, noise_in, gain_ref, out_in, gate_in,
    delta_ref, send_ref, condition_ref, added_rows_ref, small_ref, offset_ref, noise_ref, out_ref, gate_ref, sems,
):
    copies = bring((gate_in, offset_in, noise_in, out_in), (gate_ref, offset_ref, noise_ref, out_ref), sems)
    copies[0].wait()
    peers = added_ref.shape[0]
    main_rows = peers * MAIN
    gate, gate_rest = gate_ref[:main_rows, :], gate_ref[main_rows:, :]
    rest = rest_of(added_ref, NARROW)
    thirds_rest = three(gate_rest, 1).astype(F32)
    for piece in range(NARROW):
        columns = slice(piece * NARROW_PART, (piece + 1) * NARROW_PART)
        added_rows_ref[:, columns] = main_of(added_ref, piece)
        mine = jnp.where(of_part(peers * REST, piece), thirds_rest, 0.0).astype(BF16)
        condition_ref[:, columns] = direct_ref[:, columns] + of_three(matmul(mine, rest, 0, 0))
    condition_ref[...] += of_three(matmul(three(gate, 1), added_rows_ref[...], 0, 0))
    for copy in copies[1:]:
        copy.wait()
    condition = condition_ref[...]
    gain = gain_ref[...]
    head_out = out_ref[...]
    exit_thirds = jnp.concatenate([head_out, head_out, head_out], axis=0)
    loss = jnp.zeros((1, 1), F32)
    entry_grad = jnp.zeros(head_out.shape, F32)
    exit_grad = jnp.zeros(head_out.shape, F32)
    gain_grad = jnp.zeros_like(gain)
    cond_delta = jnp.zeros_like(condition)
    for draw in range(NOISE):
        state = condition + offset_ref[draw]
        centred = state - jnp.mean(state, axis=1, keepdims=True)
        inv_std = lax.rsqrt(jnp.mean(centred * centred, axis=1, keepdims=True) + NORM_EPS)
        normed = centred * inv_std
        scaled = normed * gain
        sigmoid_val = 1.0 / (1.0 + jnp.exp(-scaled))
        active = (scaled * sigmoid_val).astype(BF16)
        error = matmul(head_out, active, 1, 1) - noise_ref[draw]
        loss = loss + jnp.sum(jnp.sum(error * error, axis=1, keepdims=True), axis=0, keepdims=True)
        grad_pred = three(2.0 / NOISE * error, 0)
        exit_grad = exit_grad + of_three(matmul(grad_pred, active))
        grad_act = matmul(grad_pred, exit_thirds, 0, 0)
        grad_scaled = grad_act * sigmoid_val * (1.0 + scaled * (1.0 - sigmoid_val))
        gain_grad = gain_grad + jnp.sum(grad_scaled * normed, axis=0, keepdims=True)
        grad_normed = grad_scaled * gain
        grad_state = inv_std * (
            grad_normed
            - jnp.mean(grad_normed, axis=1, keepdims=True)
            - normed * jnp.mean(grad_normed * normed, axis=1, keepdims=True)
        )
        noisy = three(noisy_ref[draw], 0)
        high = grad_state.astype(BF16)
        left = (grad_state - high.astype(F32)).astype(BF16)
        entry_grad = entry_grad + of_three(matmul(noisy, high) + matmul(noisy, left))
        cond_delta = cond_delta + grad_state
    delta = cond_delta.astype(BF16)
    delta_ref[...] = delta

    small_ref[...] = jnp.zeros_like(small_ref)
    channels = entry_grad.shape[0]
    for block in range(HW // LANES):
        columns = slice(block * LANES, (block + 1) * LANES)
        at = block * channels
        small_ref[ENTRY_ROW + at : ENTRY_ROW + at + channels, :] = entry_grad[:, columns]
        small_ref[EXIT_ROW + at : EXIT_ROW + at + channels, :] = exit_grad[:, columns]
        small_ref[GAIN_ROW + block : GAIN_ROW + block + 1, :] = gain_grad[:, columns]
    small_ref[LOSS_ROW : LOSS_ROW + 1, :] = jnp.broadcast_to(loss, (1, LANES))
    small = two(small_ref[...].reshape(peers, small_ref.shape[0] // peers, LANES))

    pick = jnp.where(gate != 0.0, 1.0, 0.0).astype(BF16)
    pick_rest = jnp.where(gate_rest != 0.0, 1.0, 0.0)
    slot_gate = jnp.sum(gate, axis=1, keepdims=True)
    total = jnp.zeros((peers * REST, NARROW_PART), F32)
    for piece in range(NARROW):
        columns = delta[:, piece * NARROW_PART : (piece + 1) * NARROW_PART]
        main = (matmul(pick, columns) * slot_gate).astype(BF16)
        send_ref[:, MAIN * piece : MAIN * (piece + 1), :] = main.reshape(peers, MAIN, NARROW_PART)
        mine = jnp.where(of_part(peers * REST, piece), pick_rest, 0.0).astype(BF16)
        total = total + matmul(mine, columns)
    total = total * jnp.sum(gate_rest, axis=1, keepdims=True)
    tail = jnp.concatenate([total.reshape(peers, REST, NARROW_PART), small], axis=1)
    send_ref[:, MAIN * NARROW :, :] = tail.astype(BF16)


def send_back(held_ref, up_ref, send_ref, rest_ref):
    step = pl.program_id(0)
    peers = send_ref.shape[0]
    main_rows = peers * MAIN
    back = matmul(held_ref[...], up_ref[...], 1, 1).astype(BF16)

    @pl.when(step == 0)
    def _():
        rest_ref[...] = jnp.zeros_like(rest_ref)

    width = send_ref.shape[2]
    for side in range(2):
        part = 2 * step + side
        columns = slice(side * width, (side + 1) * width)
        send_ref[:, pl.ds(pl.multiple_of(part * MAIN, MAIN), MAIN), :] = back[:main_rows, columns].reshape(
            peers, MAIN, width
        )
        rest_ref[...] += matmul(rest_spread(peers, part), back[main_rows:, columns])

    @pl.when(step == WIDE // 2 - 1)
    def _():
        send_ref[:, MAIN * WIDE :, :] = rest_ref[...].reshape(peers, REST, width).astype(BF16)


def backward_kernel(
    grads_ref, mixed_in, slope_ref, up_ref, slot_ref, held_ref, small_ref, send_ref, rest_ref, mixed_ref, sem
):
    peers = grads_ref.shape[0]
    main_rows = peers * MAIN

    @pl.when(pl.program_id(0) == 0)
    def _():
        mixed_copy = pltpu.make_async_copy(mixed_in, mixed_ref, sem)
        mixed_copy.start()
        tail = grads_ref[:, MAIN * NARROW :, :].astype(F32)
        rest = flat(tail[:, :REST, :]).astype(BF16)
        for piece in range(NARROW):
            columns = slice(piece * NARROW_PART, (piece + 1) * NARROW_PART)
            slot_ref[:main_rows, columns] = main_of(grads_ref, piece)
            slot_ref[main_rows:, columns] = matmul(rest_rows(peers, piece), rest).astype(BF16)
        mixed_copy.wait()
        grad_hidden = matmul(slot_ref[...], mixed_ref[...], 1, 1)
        held_ref[...] = (grad_hidden * slope_ref[...]).astype(BF16)
        small = jnp.sum(tail[:, REST:, :], axis=0)
        small_ref[...] = small[:, :LANES] + small[:, LANES:]

    send_back(held_ref, up_ref, send_ref, rest_ref)


def second_kernel(held_ref, up_ref, send_ref, rest_ref):
    send_back(held_ref, up_ref, send_ref, rest_ref)


def cond_grad_kernel(slot_ref, hidden_ref, delta_ref, down_ref, tokens_ref, grad_ref, left_ref, right_ref):
    features = down_ref.shape[0]

    @pl.when(pl.program_id(0) == 0)
    def _():
        left_ref[:, :features] = matmul(slot_ref[...], hidden_ref[...], 0, 0).astype(BF16)
        left_ref[:, features:] = delta_ref[...].astype(F32).T.astype(BF16)

    right_ref[:features, :] = down_ref[...]
    right_ref[features:, :] = tokens_ref[...]
    total = matmul(left_ref[...], right_ref[...])
    width = grad_ref.shape[2]
    for side in range(grad_ref.shape[0]):
        grad_ref[side] = total[:, side * width : (side + 1) * width]


def grad_part(block_ref, gate_ref, tokens_ref, gain_ref, scaled_ref, first, mean):
    peers = block_ref.shape[0]
    main_rows = peers * MAIN
    pick = jnp.where(gate_ref[:main_rows, :] != 0.0, 1.0, 0.0).astype(BF16)
    pick_rest = jnp.where(gate_ref[main_rows:, :] != 0.0, 1.0, 0.0)
    rest = rest_of(block_ref, WIDE)
    width = block_ref.shape[2]
    for part in range(WIDE):
        here = slice(part * width, (part + 1) * width)
        columns = slice(first + part * width, first + (part + 1) * width)
        mine = jnp.where(of_part(peers * REST, part), pick_rest, 0.0).astype(BF16)
        total = matmul(pick, main_of(block_ref, part), 0, 0) + matmul(mine, rest, 0, 0)
        scaled = total * gain_ref[:, columns]
        scaled_ref[:, here] = scaled
        mean = mean + jnp.sum(tokens_ref[:, columns].astype(F32) * scaled, axis=1, keepdims=True)
    return mean


def front_kernel(block_ref, gate_ref, tokens_ref, gain_ref, scaled_ref, mean_ref):
    mean_ref[...] = grad_part(block_ref, gate_ref, tokens_ref, gain_ref, scaled_ref, 0, jnp.zeros_like(mean_ref))


def finish_kernel(
    block_ref, front_ref, mean_ref, gate_ref, layer_ref, tokens_ref, inverse_ref, gain_ref, grad_ref, scaled_ref
):
    half = front_ref.shape[1]
    mean = grad_part(block_ref, gate_ref, tokens_ref, gain_ref, scaled_ref, half, mean_ref[...])
    mean = mean / tokens_ref.shape[1]
    inverse = inverse_ref[...]
    cubed = inverse * inverse * inverse * mean
    first = 0
    for part_ref in (front_ref, scaled_ref):
        columns = slice(first, first + part_ref.shape[1])
        first = first + part_ref.shape[1]
        direct = inverse * part_ref[...] - tokens_ref[:, columns].astype(F32) * cubed
        grad_ref[:, columns] = (layer_ref[:, columns] + direct).astype(BF16)


def totals_kernel(sums_ref, cond_ref, entry_ref, exit_ref, gain_ref, loss_ref, total_ref, small_ref):
    dense = total_ref.shape[0]
    peers = sums_ref.shape[0]
    total_ref[...] = jnp.sum(sums_ref[:, :dense, :].astype(F32), axis=0)
    blocks = cond_ref.shape[1] // LANES
    for block in range(blocks):
        cond_ref[:, block * LANES : (block + 1) * LANES] = total_ref[pl.ds(block, dense // blocks, stride=blocks), :]
    small = sums_ref[:, dense:, :].astype(F32)
    small_ref[...] = flat(small[:, :8, :] + small[:, 8:, :])
    channels = entry_ref.shape[0]
    for block in range(blocks):
        columns = slice(block * LANES, (block + 1) * LANES)
        at = block * channels
        entry_ref[:, columns] = small_ref[ENTRY_ROW + at : ENTRY_ROW + at + channels, :]
        exit_ref[:, columns] = small_ref[EXIT_ROW + at : EXIT_ROW + at + channels, :]
        gain_ref[:, columns] = small_ref[GAIN_ROW + block : GAIN_ROW + block + 1, :]
    loss_ref[...] = small_ref[LOSS_ROW : LOSS_ROW + 1, :]


def whole(*shape):
    return pl.BlockSpec(shape, lambda *step: (0,) * len(shape))


def once(*shape):
    return pl.BlockSpec(shape, lambda *step: (0,) * len(shape), pipeline_mode=pl.Buffered(1))


def stored(shape, dtype):
    return pltpu.HBM(shape, dtype)


def shaped(shape, dtype):
    return jax.ShapeDtypeStruct(shape, dtype)


def call(kernel, grid, in_specs, out_specs, out_shape, scratch, flops, moved):
    return pl.pallas_call(
        kernel,
        grid=grid,
        in_specs=in_specs,
        out_specs=out_specs,
        out_shape=out_shape,
        scratch_shapes=scratch,
        compiler_params=pltpu.CompilerParams(vmem_limit_bytes=48 << 20),
        cost_estimate=pl.CostEstimate(flops=flops, bytes_accessed=moved, transcendentals=0),
    )


def exchange(block):
    return lax.all_to_all(block, EXPERT, split_axis=0, concat_axis=0, tiled=True)


def on_device(
    tokens,
    norm_gain,
    experts_chosen,
    gate_weights,
    expert_up,
    expert_down,
    head_cond,
    head_in,
    head_gain,
    head_out,
    latents,
    noise_draws,
    timesteps,
):
    tok_rows, width = tokens.shape
    experts = lax.axis_size(EXPERT)
    features = expert_up.shape[2]
    rows = experts * (MAIN + 2)
    slot_rows = experts * (MAIN + REST)
    less, more = LESS_PART, MORE_PART
    block_rows = WIDE * MAIN + REST
    less_block, more_block = (experts, block_rows, less), (experts, block_rows, more)
    cond_rows = head_cond.shape[0]
    joined = less_block[:1] + (block_rows + TAIL, less)
    half = HALF_PART
    half_block = (experts, block_rows, half)
    narrow_block = (experts, NARROW * MAIN + REST, NARROW_PART)
    grads_block = (experts, NARROW * MAIN + REST + 8, NARROW_PART)
    small_rows = 8
    steps = WIDE // 2
    group = 8
    gain_row = norm_gain.reshape(1, width)
    far = pl.BlockSpec(memory_space=pltpu.HBM)
    weight_up = expert_up[0]
    weight_down = expert_down[0]
    expert_flops = rows * features * width

    send, send_later, gate, inverse = call(
        dispatch_kernel,
        (experts // group,),
        [far, far, far, far, far],
        [
            pl.BlockSpec((group,) + joined[1:], lambda step: (step, 0, 0)),
            pl.BlockSpec((group,) + more_block[1:], lambda step: (step, 0, 0)),
            whole(slot_rows, tok_rows),
            whole(tok_rows, 1),
        ],
        [
            stored(joined, BF16),
            stored(more_block, BF16),
            stored((slot_rows, tok_rows), F32),
            stored((tok_rows, 1), F32),
        ],
        [
            pltpu.VMEM((tok_rows, width), BF16),
            pltpu.VMEM((tok_rows, width), BF16),
            pltpu.VMEM((1, width), F32),
            pltpu.VMEM((TOPK, tok_rows), jnp.int32),
            pltpu.VMEM((TOPK, tok_rows), F32),
            pltpu.VMEM(head_cond.shape, BF16),
            pltpu.VMEM((TAIL, less), F32),
            pltpu.SemaphoreType.DMA((5,)),
        ],
        800_000_000,
        5_000_000,
    )(tokens, gain_row, experts_chosen.T, gate_weights.T, head_cond)

    def of_draws():
        levels = signal_level(timesteps)[:, None, :]
        noisy = jnp.sqrt(levels) * latents[None] + jnp.sqrt(1.0 - levels) * noise_draws
        entered = lax.dot_general(noisy, head_in.astype(F32), (((1,), (0,)), ((), ())), precision=HIGH)
        return entered + time_embed(timesteps.reshape(-1)).reshape(NOISE, tok_rows, HW), noisy

    core = lax.axis_index("core")
    shapes = ((NOISE, tok_rows, HW), noise_draws.shape)
    early = lax.cond(core == 0, of_draws, lambda: tuple(jnp.zeros(shape, F32) for shape in shapes))

    send, early = lax.optimization_barrier((send, early))
    arrived = exchange(send)
    arrived_later = exchange(send_later)
    cond_part = arrived[:, block_rows : block_rows + NARROW * cond_rows, :]
    cond_part = cond_part.reshape(experts, NARROW, cond_rows, NARROW_PART).transpose(0, 2, 1, 3).reshape(-1, HW)
    cond_full = lax.all_gather(cond_part, DP, axis=0, tiled=True)

    down_cond = matmul(weight_down, cond_full).astype(BF16)
    direct = matmul(tokens, cond_full)

    pre_act = call(
        first_kernel,
        (steps,),
        [once(*joined), pl.BlockSpec((2 * less, features), lambda step: (step, 0))],
        whole(rows, features),
        stored((rows, features), F32),
        [pltpu.VMEM((rows, 2 * less), BF16)],
        expert_flops,
        6_000_000,
    )(arrived, weight_up)
    pre_act, hidden, send = call(
        forward_kernel,
        (steps,),
        [
            once(*more_block),
            pl.BlockSpec((2 * more, features), lambda step: (step + 1, 0)),
            far,
            far,
        ],
        [whole(rows, features), whole(rows, features), whole(*narrow_block)],
        [stored((rows, features), F32), stored((rows, features), BF16), stored(narrow_block, BF16)],
        [
            pltpu.VMEM((rows, 2 * more), BF16),
            pltpu.VMEM((rows, features), F32),
            pltpu.VMEM((features, HW), BF16),
            pltpu.SemaphoreType.DMA((2,)),
        ],
        2 * expert_flops,
        10_000_000,
    )(arrived_later, weight_up, pre_act, down_cond)
    added = exchange(send)
    offset, noisy = lax.cond(core == 1, of_draws, lambda: early)
    slope = gelu_slope(pre_act)

    delta, send = call(
        head_kernel,
        (1,),
        [
            whole(*narrow_block),
            whole(tok_rows, HW),
            far,
            whole(*noisy.shape),
            far,
            whole(1, HW),
            far,
            far,
        ],
        [whole(tok_rows, HW), whole(*grads_block)],
        [stored((tok_rows, HW), BF16), stored(grads_block, BF16)],
        [
            pltpu.VMEM((tok_rows, HW), F32),
            pltpu.VMEM((experts * MAIN, HW), BF16),
            pltpu.VMEM((experts * small_rows, LANES), F32),
            pltpu.VMEM((NOISE, tok_rows, HW), F32),
            pltpu.VMEM(noise_draws.shape, F32),
            pltpu.VMEM(head_out.shape, BF16),
            pltpu.VMEM((slot_rows, tok_rows), F32),
            pltpu.SemaphoreType.DMA((4,)),
        ],
        1_500_000_000,
        5_000_000,
    )(added, direct, offset, noisy, noise_draws, head_gain.reshape(1, HW), head_out, gate)
    arrived = exchange(send)

    slot_grads, held, small, send = call(
        backward_kernel,
        (steps,),
        [
            once(*grads_block),
            far,
            once(rows, features),
            pl.BlockSpec((2 * half, features), lambda step: (step, 0)),
        ],
        [whole(rows, HW), whole(rows, features), whole(small_rows, LANES), whole(*half_block)],
        [
            stored((rows, HW), BF16),
            stored((rows, features), BF16),
            stored((small_rows, LANES), F32),
            stored(half_block, BF16),
        ],
        [
            pltpu.VMEM((experts * REST, half), F32),
            pltpu.VMEM((features, HW), BF16),
            pltpu.SemaphoreType.DMA,
        ],
        2 * expert_flops,
        10_000_000,
    )(arrived, down_cond, slope, weight_up)
    slot_grads, held, small, send = lax.optimization_barrier((slot_grads, held, small, send))
    front = exchange(send)
    send = call(
        second_kernel,
        (steps,),
        [once(rows, features), pl.BlockSpec((2 * half, features), lambda step: (step + steps, 0))],
        whole(*half_block),
        stored(half_block, BF16),
        [pltpu.VMEM((experts * REST, half), F32)],
        0,
        0,
    )(held, weight_up)

    back = exchange(send)

    chunks = lax.axis_size(DP)
    chunk = width // chunks
    cond_grad = call(
        cond_grad_kernel,
        (chunks // 2,),
        [
            once(rows, HW),
            once(rows, features),
            once(tok_rows, HW),
            pl.BlockSpec((features, 2 * chunk), lambda step: (0, step)),
            pl.BlockSpec((tok_rows, 2 * chunk), lambda step: (0, step)),
        ],
        pl.BlockSpec((2, HW, chunk), lambda step: (step, 0, 0)),
        stored((chunks, HW, chunk), F32),
        [pltpu.VMEM((HW, features + tok_rows), BF16), pltpu.VMEM((features + tok_rows, 2 * chunk), BF16)],
        0,
        0,
    )(slot_grads, hidden, delta, weight_down, tokens)
    cond_grad = lax.psum_scatter(cond_grad, DP, scatter_dimension=0, tiled=True)[0]
    small, front = lax.optimization_barrier((small, front))
    small = lax.all_gather(small, DP, axis=0, tiled=True)
    small = jnp.sum(small.reshape(-1, small_rows, LANES), axis=0)
    high = lax.reduce_precision(small, 8, 7)
    small = jnp.concatenate([high, small - high], axis=0).astype(BF16)
    cond_grad = cond_grad.T.astype(BF16).reshape(experts, -1, LANES)
    dense = cond_grad.shape[1]
    sums = jnp.concatenate([cond_grad, jnp.broadcast_to(small[None], (experts,) + small.shape)], axis=1)

    grad_layer = matmul(delta, cond_full, 1, 1)
    scaled_front, mean_front = call(
        front_kernel,
        (1,),
        [whole(*half_block), whole(slot_rows, tok_rows), whole(tok_rows, width), whole(1, width)],
        [whole(tok_rows, WIDE * half), whole(tok_rows, 1)],
        [shaped((tok_rows, WIDE * half), F32), shaped((tok_rows, 1), F32)],
        [],
        1_000_000_000,
        6_000_000,
    )(front, gate, tokens, gain_row)
    input_grad = call(
        finish_kernel,
        (1,),
        [
            whole(*half_block),
            whole(tok_rows, WIDE * half),
            whole(tok_rows, 1),
            whole(slot_rows, tok_rows),
            whole(tok_rows, width),
            whole(tok_rows, width),
            whole(tok_rows, 1),
            whole(1, width),
        ],
        whole(tok_rows, width),
        shaped((tok_rows, width), BF16),
        [pltpu.VMEM((tok_rows, WIDE * half), F32)],
        1_000_000_000,
        8_000_000,
    )(back, scaled_front, mean_front, gate, grad_layer, tokens, inverse, gain_row)
    sums = exchange(sums)
    cond_grad, entry_grad, exit_grad, gain_grad, loss_sum = call(
        totals_kernel,
        (1,),
        [whole(*sums.shape)],
        [
            whole(*head_cond.shape),
            whole(*head_in.shape),
            whole(*head_out.shape),
            whole(1, HW),
            whole(1, LANES),
        ],
        [
            shaped(head_cond.shape, F32),
            shaped(head_in.shape, F32),
            shaped(head_out.shape, F32),
            shaped((1, HW), F32),
            shaped((1, LANES), F32),
        ],
        [pltpu.VMEM((dense, LANES), F32), pltpu.VMEM((experts * small_rows, LANES), F32)],
        1_000_000,
        1_000_000,
    )(sums)

    mean_loss = loss_sum[0, 0] / (tok_rows * lax.axis_size(EVERY) * NOISE)
    return (input_grad, cond_grad, entry_grad, exit_grad, gain_grad[0], mean_loss)


def solution(mesh):
    shape = (mesh.shape["dp"] // CORES, CORES, mesh.shape["expert"] // RING, RING)
    fine = Mesh(mesh.devices.reshape(shape), EVERY)
    return jax.shard_map(
        on_device,
        mesh=fine,
        in_specs=(
            P(EVERY, None),
            P(),
            P(EVERY, None),
            P(EVERY, None),
            P(EXPERT, None, None),
            P(EXPERT, None, None),
            P(EVERY, None),
            P(),
            P(),
            P(),
            P(None, EVERY),
            P(None, None, EVERY),
            P(None, EVERY),
        ),
        out_specs=(P(EVERY, None), P(EVERY, None), P(), P(), P(), P()),
        check_vma=False,
    )
```

profile of v0, /device:TPU:36, one launch (start us, length us, event | category | flops | bytes accessed | tf_op | source)
XLA Modules:
  0.0 329.3 jit_solution(17536308436099379704)
XLA Ops:
  7.3 8.6 %conditional.2 = (f32[4,128,768]{2,1,0:T(8,128)}, f32[4,16,128]{2,1,0:T(8,128)}) conditional(s32[]{:T(128)} %convert_element_type.43, () %tuple.25, (s32[4,128]{1,0:T(4,128)}, f32[16,128]{1,0:T(8,128)}, f32[4,16,128]{2,1,0:T(8,128)}, bf16[16,768]{1,0:T(8,128)(2,1)}) %tuple.26), branch_computations={%region_0.0_spmd, %region_1.0_spmd} | conditional | flops 76509056 | bytes 4869136 | solution.py:581
  15.9 4.2 %shard_map.172 = (bf16[32,112,256]{2,1,0:T(8,128)(2,1)}, bf16[32,72,512]{2,1,0:T(8,128)(2,1)}, f32[768,128]{1,0:T(8,128)}, f32[128,1]{1,0:T(8,128)}) custom-call(bf16[128,3072]{1,0:T(8,128)(2,1)S(1)} %copy-done.1, f32[1,3072]{1,0:T(1,128)S(1)} %bitcast.42, s32[4,128]{1,0:T(4,128)S(1)} %bitcast.45, f32[4,128]{1,0:T(4,128)S(1)} %bitcast.46, ...), custom_call_target="tpu_custom_call" | custom-call | flops 800000000 | bytes 5000000 | tf_op jit(solution)/shard_map/pallas_call | solution.py:543
  20.1 50.3 %all_to_all.35.rows_ref = bf16[32,112,256]{2,1,0:T(8,128)(2,1)S(1)} all-to-all(bf16[32,112,256]{2,1,0:T(8,128)(2,1)} %get-tuple-element.67), channel_id=1, replica_groups=mesh['x'=4,'core'=2,'y'=4,'z'=8] {'y','z'}, dimensions={0} | all-to-all | bytes 3670016 | tf_op jit(solution)/shard_map/all_to_all | solution.py:502
  72.1 5.1 %all-to-all-start = ((bf16[32,72,512]{2,1,0:T(8,128)(2,1)}), bf16[32,72,512]{2,1,0:T(8,128)(2,1)}, u32[]{:S(2)}, u32[]{:S(2)}) async-start(bf16[32,72,512]{2,1,0:T(8,128)(2,1)} %get-tuple-element.63), calls=%async_computation | async-start | bytes 4718592 | tf_op jit(solution)/shard_map/all_to_all | solution.py:502
  81.2 22.9 %all-gather.2.cloned.1.call-done = bf16[3072,768]{1,0:T(8,128)(2,1)} async-done(((bf16[384,768]{1,0:T(8,128)(2,1)}), bf16[3072,768]{1,0:T(8,128)(2,1)}) %all-gather.2.cloned.1.call-update) | async-done | bytes 4718608 | tf_op jit(solution)/shard_map/all_gather | solution.py:588
  104.1 8.7 %fusion.9.mixed_in = bf16[768,768]{1,0:T(8,128)(2,1)} fusion(bf16[3072,768]{1,0:T(8,128)(2,1)} %all-gather.2.cloned.1.call-done, bf16[1,768,3072]{2,1,0:T(8,128)(2,1)} %param.22), kind=kOutput, calls=%fused_computation.26 | convolution fusion | flops 3624468480 | bytes 10616832 | tf_op jit(solution)/shard_map/dot_general | solution.py:70
  112.7 13.8 %all-to-all-done.rows_ref = bf16[32,72,512]{2,1,0:T(8,128)(2,1)} async-done(((bf16[32,72,512]{2,1,0:T(8,128)(2,1)}), bf16[32,72,512]{2,1,0:T(8,128)(2,1)}, u32[]{:S(2)}, u32[]{:S(2)}) %all-to-all-start) | async-done | bytes 2359328 | tf_op jit(solution)/shard_map/all_to_all | solution.py:502
  127.8 9.0 %shard_map.174 = (f32[576,768]{1,0:T(8,128)}, bf16[576,768]{1,0:T(8,128)(2,1)}, bf16[32,56,256]{2,1,0:T(8,128)(2,1)}) custom-call(bf16[32,72,512]{2,1,0:T(8,128)(2,1)} %all-to-all-done.rows_ref, bf16[3072,768]{1,0:T(8,128)(2,1)} %bitcast.39, f32[576,768]{1,0:T(8,128)S(1)} %copy-done.4, bf16[768,768]{1,0:T(8,128)(2,1)S(1)} %copy-done.18), custom_call_target="tpu_custom_call" | custom-call | flops 2717908992 | bytes 10000000 | tf_op jit(solution)/shard_map/pallas_call | solution.py:603
  136.8 6.1 %all-to-all-start.2 = ((bf16[32,56,256]{2,1,0:T(8,128)(2,1)}), bf16[32,56,256]{2,1,0:T(8,128)(2,1)S(1)}, u32[]{:S(2)}, u32[]{:S(2)}) async-start(bf16[32,56,256]{2,1,0:T(8,128)(2,1)} %get-tuple-element.68), calls=%async_computation.2 | async-start | bytes 1835008 | tf_op jit(solution)/shard_map/all_to_all | solution.py:502
  146.4 15.1 %all-to-all-done.2.added_ref = bf16[32,56,256]{2,1,0:T(8,128)(2,1)S(1)} async-done(((bf16[32,56,256]{2,1,0:T(8,128)(2,1)}), bf16[32,56,256]{2,1,0:T(8,128)(2,1)S(1)}, u32[]{:S(2)}, u32[]{:S(2)}) %all-to-all-start.2) | async-done | bytes 917536 | tf_op jit(solution)/shard_map/all_to_all | solution.py:502
  161.5 6.1 %shard_map.175 = (bf16[128,768]{1,0:T(8,128)(2,1)}, bf16[32,64,256]{2,1,0:T(8,128)(2,1)}) custom-call(bf16[32,56,256]{2,1,0:T(8,128)(2,1)S(1)} %all-to-all-done.2.added_ref, f32[128,768]{1,0:T(8,128)S(1)} %convolution_bitcast_fusion.direct_ref, f32[4,128,768]{2,1,0:T(8,128)} %get-tuple-element.71.offset_in, f32[4,16,128]{2,1,0:T(8,128)} %get-tuple-element.72.noisy_ref, ...), custom_call_target="tpu_custom_call" | custom-call | flops 1500000000 | bytes 5000000 | tf_op jit(solution)/shard_map/pallas_call | solution.py:627
  167.6 5.3 %all-to-all-start.3 = ((bf16[32,64,256]{2,1,0:T(8,128)(2,1)}), bf16[32,64,256]{2,1,0:T(8,128)(2,1)}, u32[]{:S(2)}, u32[]{:S(2)}) async-start(bf16[32,64,256]{2,1,0:T(8,128)(2,1)} %get-tuple-element.74), calls=%async_computation.3 | async-start | bytes 2097152 | tf_op jit(solution)/shard_map/all_to_all | solution.py:502
  175.5 18.6 %all-to-all-done.3.grads_ref = bf16[32,64,256]{2,1,0:T(8,128)(2,1)} async-done(((bf16[32,64,256]{2,1,0:T(8,128)(2,1)}), bf16[32,64,256]{2,1,0:T(8,128)(2,1)}, u32[]{:S(2)}, u32[]{:S(2)}) %all-to-all-start.3) | async-done | bytes 1048608 | tf_op jit(solution)/shard_map/all_to_all | solution.py:502
  195.3 7.6 %shard_map.176 = (bf16[576,768]{1,0:T(8,128)(2,1)}, bf16[576,768]{1,0:T(8,128)(2,1)}, f32[8,128]{1,0:T(8,128)}, bf16[32,72,384]{2,1,0:T(8,128)(2,1)}) custom-call(bf16[32,64,256]{2,1,0:T(8,128)(2,1)} %all-to-all-done.3.grads_ref, bf16[768,768]{1,0:T(8,128)(2,1)S(1)} %copy-done.19, f32[576,768]{1,0:T(8,128)S(1)} %fusion.8.slope_ref, bf16[3072,768]{1,0:T(8,128)(2,1)} %bitcast.40), custom_call_target="tpu_custom_call" | custom-call | flops 2717908992 | bytes 10000000 | tf_op jit(solution)/shard_map/pallas_call | solution.py:657
  204.2 10.3 %shard_map.180 = f32[8,768,384]{2,1,0:T(8,128)} custom-call(bf16[576,768]{1,0:T(8,128)(2,1)S(1)} %copy-done.7, bf16[576,768]{1,0:T(8,128)(2,1)S(1)} %copy-done.6, bf16[128,768]{1,0:T(8,128)(2,1)S(1)} %copy-done.8, bf16[768,3072]{1,0:T(8,128)(2,1)} %bitcast.48, bf16[128,3072]{1,0:T(8,128)(2,1)S(1)} %copy-done.1), custom_call_target="tpu_custom_call" | custom-call | tf_op jit(solution)/shard_map/pallas_call | solution.py:698
  214.5 5.3 %all-to-all-start.5 = ((bf16[32,72,384]{2,1,0:T(8,128)(2,1)}), bf16[32,72,384]{2,1,0:T(8,128)(2,1)S(1)}, u32[]{:S(2)}, u32[]{:S(2)}) async-start(bf16[32,72,384]{2,1,0:T(8,128)(2,1)} %get-tuple-element.78), calls=%async_computation.5 | async-start | bytes 3538944 | tf_op jit(solution)/shard_map/all_to_all | solution.py:502
  222.2 4.0 %shard_map.177 = bf16[32,72,384]{2,1,0:T(8,128)(2,1)} custom-call(bf16[576,768]{1,0:T(8,128)(2,1)S(1)} %copy-done.5, bf16[3072,768]{1,0:T(8,128)(2,1)S(1)} %bitcast.41), custom_call_target="tpu_custom_call" | custom-call | tf_op jit(solution)/shard_map/pallas_call | solution.py:683
  226.2 29.9 %all-to-all-done.5.block_ref = bf16[32,72,384]{2,1,0:T(8,128)(2,1)S(1)} async-done(((bf16[32,72,384]{2,1,0:T(8,128)(2,1)}), bf16[32,72,384]{2,1,0:T(8,128)(2,1)S(1)}, u32[]{:S(2)}, u32[]{:S(2)}) %all-to-all-start.5) | async-done | bytes 1769504 | tf_op jit(solution)/shard_map/all_to_all | solution.py:502
  257.3 5.4 %all-to-all-start.4 = ((bf16[32,72,384]{2,1,0:T(8,128)(2,1)}), bf16[32,72,384]{2,1,0:T(8,128)(2,1)S(1)}, u32[]{:S(2)}, u32[]{:S(2)}) async-start(bf16[32,72,384]{2,1,0:T(8,128)(2,1)} %shard_map.177), calls=%async_computation.4 | async-start | bytes 3538944 | tf_op jit(solution)/shard_map/all_to_all | solution.py:502
  262.7 12.0 %all_gather.7 = f32[64,128]{1,0:T(8,128)S(1)} all-gather(f32[8,128]{1,0:T(8,128)S(1)} %copy-done.24), channel_id=1, replica_groups=mesh['x'=4,'core'=2,'y'=4,'z'=8] {'x','core'}, dimensions={0}, use_global_device_ids=true | all-gather | bytes 36864 | tf_op jit(solution)/shard_map/all_gather | solution.py:716
  279.7 19.2 %all-to-all-done.4.block_ref = bf16[32,72,384]{2,1,0:T(8,128)(2,1)S(1)} async-done(((bf16[32,72,384]{2,1,0:T(8,128)(2,1)}), bf16[32,72,384]{2,1,0:T(8,128)(2,1)S(1)}, u32[]{:S(2)}, u32[]{:S(2)}) %all-to-all-start.4) | async-done | bytes 1769504 | tf_op jit(solution)/shard_map/all_to_all | solution.py:502
  298.9 5.4 %all-to-all-start.6 = ((bf16[32,88,128]{2,1,0:T(8,128)(2,1)}), bf16[32,88,128]{2,1,0:T(8,128)(2,1)S(1)}, u32[]{:S(2)}, u32[]{:S(2)}) async-start(bf16[32,88,128]{2,1,0:T(8,128)(2,1)} %pad_maximum_fusion), calls=%async_computation.7 | async-start | bytes 1441792 | tf_op jit(solution)/shard_map/all_to_all | solution.py:502
  304.4 4.1 %fusion.12.layer_ref = f32[128,3072]{1,0:T(8,128)S(1)} fusion(bf16[128,768]{1,0:T(8,128)(2,1)S(1)} %copy-done.9, bf16[3072,768]{1,0:T(8,128)(2,1)} %all-gather.2.cloned.1.call-done), kind=kOutput, calls=%fused_computation.36 | convolution fusion | flops 603979776 | bytes 6488064 | tf_op jit(solution)/shard_map/dot_general | solution.py:70
  311.3 8.6 %all-to-all-done.6.sums_ref = bf16[32,88,128]{2,1,0:T(8,128)(2,1)S(1)} async-done(((bf16[32,88,128]{2,1,0:T(8,128)(2,1)}), bf16[32,88,128]{2,1,0:T(8,128)(2,1)S(1)}, u32[]{:S(2)}, u32[]{:S(2)}) %all-to-all-start.6) | async-done | bytes 720928 | tf_op jit(solution)/shard_map/all_to_all | solution.py:502
  (84 shorter events, 36.7 us)
Async XLA Ops:
  7.2 96.9 %all-gather.2.cloned.1.call-start = ((), (), s32[]{:S(2)}) async-start(), calls=%async_computation.8 | async-start | bytes 5308416 | tf_op jit(solution)/shard_map/all_gather | solution.py:588
  7.2 8.6 %copy-start.1 = (bf16[128,3072]{1,0:T(8,128)(2,1)S(1)}, bf16[128,3072]{1,0:T(8,128)(2,1)}, u32[]{:S(2)}) copy-start(bf16[128,3072]{1,0:T(8,128)(2,1)} %tokens_ref.5) | copy-start | bytes 2359300
  7.2 8.6 %copy-start.13 = (f32[3072]{0:T(1024)S(1)}, f32[3072]{0:T(1024)}, u32[]{:S(2)}) copy-start(f32[3072]{0:T(1024)} %param.18) | copy-start | bytes 36868
  7.2 8.6 %copy-start.14 = (bf16[12,768]{1,0:T(8,128)(2,1)S(1)}, bf16[12,768]{1,0:T(8,128)(2,1)}, u32[]{:S(2)}) copy-start(bf16[12,768]{1,0:T(8,128)(2,1)} %cond_in.1) | copy-start | bytes 55300
  7.2 8.6 %copy-start.16 = (s32[128,4]{0,1:T(4,128)S(1)}, s32[128,4]{0,1:T(4,128)}, u32[]{:S(2)}) copy-start(s32[128,4]{0,1:T(4,128)} %param.19) | copy-start | bytes 6148
  7.3 8.6 %copy-start.17 = (f32[128,4]{0,1:T(4,128)S(1)}, f32[128,4]{0,1:T(4,128)}, u32[]{:S(2)}) copy-start(f32[128,4]{0,1:T(4,128)} %param.20) | copy-start | bytes 6148
  72.1 54.4 %all-to-all-start = ((bf16[32,72,512]{2,1,0:T(8,128)(2,1)}), bf16[32,72,512]{2,1,0:T(8,128)(2,1)}, u32[]{:S(2)}, u32[]{:S(2)}) async-start(bf16[32,72,512]{2,1,0:T(8,128)(2,1)} %get-tuple-element.63), calls=%async_computation | async-start | bytes 4718592 | tf_op jit(solution)/shard_map/all_to_all | solution.py:502
  81.2 45.3 %copy-start.4 = (f32[576,768]{1,0:T(8,128)S(1)}, f32[576,768]{1,0:T(8,128)}, u32[]{:S(2)}) copy-start(f32[576,768]{1,0:T(8,128)} %shard_map.173.start_in) | copy-start | bytes 5308420
  136.7 6.1 %copy-start.20 = (f32[4,16,128]{2,1,0:T(8,128)S(1)}, f32[4,16,128]{2,1,0:T(8,128)}, u32[]{:S(2)}) copy-start(f32[4,16,128]{2,1,0:T(8,128)} %noise_in.1) | copy-start | bytes 98308
  136.7 6.1 %copy-start.21 = (bf16[16,768]{1,0:T(8,128)(2,1)S(1)}, bf16[16,768]{1,0:T(8,128)(2,1)}, u32[]{:S(2)}) copy-start(bf16[16,768]{1,0:T(8,128)(2,1)} %param.24) | copy-start | bytes 73732
  136.8 6.1 %copy-start.22 = (f32[16,128]{1,0:T(8,128)S(1)}, f32[16,128]{1,0:T(8,128)}, u32[]{:S(2)}) copy-start(f32[16,128]{1,0:T(8,128)} %param.27) | copy-start | bytes 24580
  136.8 6.1 %copy-start.23 = (s32[4,128]{1,0:T(4,128)S(1)}, s32[4,128]{1,0:T(4,128)}, u32[]{:S(2)}) copy-start(s32[4,128]{1,0:T(4,128)} %param.29) | copy-start | bytes 6148
  136.8 24.7 %all-to-all-start.2 = ((bf16[32,56,256]{2,1,0:T(8,128)(2,1)}), bf16[32,56,256]{2,1,0:T(8,128)(2,1)S(1)}, u32[]{:S(2)}, u32[]{:S(2)}) async-start(bf16[32,56,256]{2,1,0:T(8,128)(2,1)} %get-tuple-element.68), calls=%async_computation.2 | async-start | bytes 1835008 | tf_op jit(solution)/shard_map/all_to_all | solution.py:502
  143.2 18.3 %copy-start.10 = (f32[768,128]{1,0:T(8,128)S(1)}, f32[768,128]{1,0:T(8,128)}, u32[]{:S(2)}) copy-start(f32[768,128]{1,0:T(8,128)} %get-tuple-element.73.gate_in.gate_ref) | copy-start | bytes 1179652
  143.2 18.3 %copy-start.15 = (bf16[16,768]{1,0:T(8,128)(2,1)S(1)}, bf16[16,768]{1,0:T(8,128)(2,1)}, u32[]{:S(2)}) copy-start(bf16[16,768]{1,0:T(8,128)(2,1)} %out_in.1) | copy-start | bytes 73732
  167.6 26.4 %all-to-all-start.3 = ((bf16[32,64,256]{2,1,0:T(8,128)(2,1)}), bf16[32,64,256]{2,1,0:T(8,128)(2,1)}, u32[]{:S(2)}, u32[]{:S(2)}) async-start(bf16[32,64,256]{2,1,0:T(8,128)(2,1)} %get-tuple-element.74), calls=%async_computation.3 | async-start | bytes 2097152 | tf_op jit(solution)/shard_map/all_to_all | solution.py:502
  172.9 101.8 %reduce-scatter.2.cloned.1.call-start = ((), (), s32[]{:S(2)}) async-start(), calls=%async_computation.9 | async-start | bytes 10616832 | tf_op jit(solution)/shard_map/reduce_scatter | solution.py:714
  175.5 27.5 %copy-start.6 = (bf16[576,768]{1,0:T(8,128)(2,1)S(1)}, bf16[576,768]{1,0:T(8,128)(2,1)}, u32[]{:S(2)}) copy-start(bf16[576,768]{1,0:T(8,128)(2,1)} %get-tuple-element.85.hidden_ref) | copy-start | bytes 2654212
  195.3 7.7 %copy-start.8 = (bf16[128,768]{1,0:T(8,128)(2,1)S(1)}, bf16[128,768]{1,0:T(8,128)(2,1)}, u32[]{:S(2)}) copy-start(bf16[128,768]{1,0:T(8,128)(2,1)} %get-tuple-element.82.delta_ref) | copy-start | bytes 589828
  214.5 41.5 %all-to-all-start.5 = ((bf16[32,72,384]{2,1,0:T(8,128)(2,1)}), bf16[32,72,384]{2,1,0:T(8,128)(2,1)S(1)}, u32[]{:S(2)}, u32[]{:S(2)}) async-start(bf16[32,72,384]{2,1,0:T(8,128)(2,1)} %get-tuple-element.78), calls=%async_computation.5 | async-start | bytes 3538944 | tf_op jit(solution)/shard_map/all_to_all | solution.py:502
  226.2 36.5 %copy-start.24 = (f32[8,128]{1,0:T(8,128)S(1)}, f32[8,128]{1,0:T(8,128)}, u32[]{:S(2)}) copy-start(f32[8,128]{1,0:T(8,128)} %get-tuple-element.86) | copy-start | bytes 12292
  257.3 41.6 %all-to-all-start.4 = ((bf16[32,72,384]{2,1,0:T(8,128)(2,1)}), bf16[32,72,384]{2,1,0:T(8,128)(2,1)S(1)}, u32[]{:S(2)}, u32[]{:S(2)}) async-start(bf16[32,72,384]{2,1,0:T(8,128)(2,1)} %shard_map.177), calls=%async_computation.4 | async-start | bytes 3538944 | tf_op jit(solution)/shard_map/all_to_all | solution.py:502
  278.8 25.6 %copy-start.9 = (bf16[128,768]{1,0:T(8,128)(2,1)S(1)}, bf16[128,768]{1,0:T(8,128)(2,1)}, u32[]{:S(2)}) copy-start(bf16[128,768]{1,0:T(8,128)(2,1)} %get-tuple-element.82.delta_ref) | copy-start | bytes 589828
  298.9 21.0 %all-to-all-start.6 = ((bf16[32,88,128]{2,1,0:T(8,128)(2,1)}), bf16[32,88,128]{2,1,0:T(8,128)(2,1)S(1)}, u32[]{:S(2)}, u32[]{:S(2)}) async-start(bf16[32,88,128]{2,1,0:T(8,128)(2,1)} %pad_maximum_fusion), calls=%async_computation.7 | async-start | bytes 1441792 | tf_op jit(solution)/shard_map/all_to_all | solution.py:502
  (10 other events, 27.9 us)
Sparse Core Ops, SparseCore 0:
  72.2 31.8 all-gather.1
  214.6 54.2 reduce-scatter.1
where the time goes:
time: 331 us; the launch traced here: 329 us
  waiting for transfers between devices  128 us (39%)
  blocking collectives  62.3 us (19%)
  Pallas kernels  48.7 us (15%)
  starting transfers between devices  32.8 us (10%)
  matrix products  18.8 us (6%)
  between operations  15.7 us (5%)
  local copies, waits for them, and re-layouts  11.8 us (4%)
  other arithmetic  11.1 us (3%)
    all_to_all x6, waiting for transfers between devices, exchange(): lax.all_to_all(block, EXPERT, split_axis=0, concat_axis=0, tiled=True)  105 us
    all_to_all x1, blocking collectives, exchange(): lax.all_to_all(block, EXPERT, split_axis=0, concat_axis=0, tiled=True)  50.3 us
    all_to_all x6, starting transfers between devices, exchange(): lax.all_to_all(block, EXPERT, split_axis=0, concat_axis=0, tiled=True)  32.7 us
    all_gather x1, waiting for transfers between devices, on_device(): cond_full = lax.all_gather(cond_part, DP, axis=0, tiled=True)  22.9 us
    dot_general x3, matrix products, matmul(): lax.dot_general(left, right, (((left_dim,), (right_dim,)), ((), ())), pre...  16 us
    all_gather x1, blocking collectives, on_device(): small = lax.all_gather(small, DP, axis=0, tiled=True)  12 us
    pallas_call x1, Pallas kernels, on_device(): call(cond_grad_kernel, (chunks // 2,), [once(rows, HW), once(rows, featur...  10.3 us
    pallas_call x1, Pallas kernels, on_device(): call(forward_kernel, (steps,), [once(*more_block), pl.BlockSpec((2 * more...  8.96 us
  transfers between devices with their start and end apart: 8, of which 7 were waited for; matrix products, arithmetic and copies ran while one was open for 7% of the time, Pallas kernels for 3%

commit v1 on v0

--- a/solution.py
+++ b/solution.py
@@ -396,20 +396,13 @@
     send_back(held_ref, up_ref, send_ref, rest_ref)
 
 
-def cond_grad_kernel(slot_ref, hidden_ref, delta_ref, down_ref, tokens_ref, grad_ref, left_ref, right_ref):
-    features = down_ref.shape[0]
-
+def cond_grad_kernel(hidden_ref, slot_ref, down_ref, tokens_ref, delta_ref, grad_ref, both_ref):
     @pl.when(pl.program_id(0) == 0)
     def _():
-        left_ref[:, :features] = matmul(slot_ref[...], hidden_ref[...], 0, 0).astype(BF16)
-        left_ref[:, features:] = delta_ref[...].astype(F32).T.astype(BF16)
-
-    right_ref[:features, :] = down_ref[...]
-    right_ref[features:, :] = tokens_ref[...]
-    total = matmul(left_ref[...], right_ref[...])
-    width = grad_ref.shape[2]
-    for side in range(grad_ref.shape[0]):
-        grad_ref[side] = total[:, side * width : (side + 1) * width]
+        both_ref[...] = matmul(hidden_ref[...], slot_ref[...], 0, 0).astype(BF16)
+
+    total = matmul(down_ref[...], both_ref[...], 0, 0) + matmul(tokens_ref[...], delta_ref[...], 0, 0)
+    grad_ref[...] = total.astype(BF16)
 
 
 def grad_part(block_ref, gate_ref, tokens_ref, gain_ref, scaled_ref, first, mean):
@@ -457,8 +450,10 @@
     blocks = cond_ref.shape[1] // LANES
     for block in range(blocks):
         cond_ref[:, block * LANES : (block + 1) * LANES] = total_ref[pl.ds(block, dense // blocks, stride=blocks), :]
-    small = sums_ref[:, dense:, :].astype(F32)
-    small_ref[...] = flat(small[:, :8, :] + small[:, 8:, :])
+    for line in range((sums_ref.shape[1] - dense) // 16):
+        first = dense + line * 16
+        small = sums_ref[:, first : first + 16, :].astype(F32)
+        small_ref[line * peers * 8 : (line + 1) * peers * 8, :] = flat(small[:, :8, :] + small[:, 8:, :])
     channels = entry_ref.shape[0]
     for block in range(blocks):
         columns = slice(block * LANES, (block + 1) * LANES)
@@ -693,33 +688,35 @@
 
     back = exchange(send)
 
-    chunks = lax.axis_size(DP)
-    chunk = width // chunks
+    block = 512
     cond_grad = call(
         cond_grad_kernel,
-        (chunks // 2,),
-        [
+        (width // block,),
+        [
+            once(rows, features),
             once(rows, HW),
-            once(rows, features),
+            pl.BlockSpec((features, block), lambda step: (0, step)),
+            pl.BlockSpec((tok_rows, block), lambda step: (0, step)),
             once(tok_rows, HW),
-            pl.BlockSpec((features, 2 * chunk), lambda step: (0, step)),
-            pl.BlockSpec((tok_rows, 2 * chunk), lambda step: (0, step)),
-        ],
-        pl.BlockSpec((2, HW, chunk), lambda step: (step, 0, 0)),
-        stored((chunks, HW, chunk), F32),
-        [pltpu.VMEM((HW, features + tok_rows), BF16), pltpu.VMEM((features + tok_rows, 2 * chunk), BF16)],
+        ],
+        pl.BlockSpec((block, HW), lambda step: (step, 0)),
+        stored((width, HW), BF16),
+        [pltpu.VMEM((features, HW), BF16)],
         0,
         0,
-    )(slot_grads, hidden, delta, weight_down, tokens)
-    cond_grad = lax.psum_scatter(cond_grad, DP, scatter_dimension=0, tiled=True)[0]
+    )(hidden, slot_grads, weight_down, tokens, delta)
+    cond_grad = lax.psum_scatter(cond_grad, DP, scatter_dimension=0, tiled=True).astype(F32)
+    cond_grad = lax.psum_scatter(cond_grad, "y", scatter_dimension=0, tiled=True)
     small, front = lax.optimization_barrier((small, front))
     small = lax.all_gather(small, DP, axis=0, tiled=True)
     small = jnp.sum(small.reshape(-1, small_rows, LANES), axis=0)
     high = lax.reduce_precision(small, 8, 7)
     small = jnp.concatenate([high, small - high], axis=0).astype(BF16)
-    cond_grad = cond_grad.T.astype(BF16).reshape(experts, -1, LANES)
+    small = lax.all_gather(small, "y", axis=0, tiled=True)
+    ring = lax.axis_size("z")
+    cond_grad = cond_grad.astype(BF16).reshape(ring, -1, LANES)
     dense = cond_grad.shape[1]
-    sums = jnp.concatenate([cond_grad, jnp.broadcast_to(small[None], (experts,) + small.shape)], axis=1)
+    sums = jnp.concatenate([cond_grad, jnp.broadcast_to(small[None], (ring,) + small.shape)], axis=1)
 
     grad_layer = matmul(delta, cond_full, 1, 1)
     scaled_front, mean_front = call(
@@ -751,7 +748,7 @@
         1_000_000_000,
         8_000_000,
     )(back, scaled_front, mean_front, gate, grad_layer, tokens, inverse, gain_row)
-    sums = exchange(sums)
+    sums = lax.all_to_all(sums, "z", split_axis=0, concat_axis=0, tiled=True)
     cond_grad, entry_grad, exit_grad, gain_grad, loss_sum = call(
         totals_kernel,
         (1,),

time: 331 us -> 327 us (0.988)
  waiting for transfers between devices: 128 us -> 113 us
  blocking collectives: 62.3 us -> 75.4 us
    all_to_all x6 -> x5, waiting for transfers between devices: 105 us -> 80.5 us  [exchange(): lax.all_to_all(block, EXPERT, split_axis=0, concat_axis=0, tiled=True)]
    all_gather x0 -> x1, blocking collectives: none -> 13.5 us  [on_device(): small = lax.all_gather(small, 'y', axis=0, tiled=True)]
    all_to_all x0 -> x1, starting transfers between devices: none -> 6.18 us  [on_device(): sums = lax.all_to_all(sums, 'z', split_axis=0, concat_axis=0, tiled=True)]
    all_to_all x6 -> x5, starting transfers between devices: 32.7 us -> 27.2 us  [exchange(): lax.all_to_all(block, EXPERT, split_axis=0, concat_axis=0, tiled=True)]
    reduce_scatter x1 -> x2, waiting for transfers between devices: 0.02 us -> 5.11 us  [the longest x1 5.09 us: on_device(): lax.psum_scatter(cond_grad, 'y', scatter_dimension=0, tiled=True)]
    all_to_all x0 -> x1, waiting for transfers between devices: none -> 3.66 us  [on_device(): sums = lax.all_to_all(sums, 'z', split_axis=0, concat_axis=0, tiled=True)]
  transfers between devices with their start and end apart: 8 -> 9, of which waited for: 7 -> 8; matrix products, arithmetic and copies ran while one was open for 7% -> 6% of each run, Pallas kernels for 3% -> 3%
where the time goes in v1:
time: 327 us; the launch traced here: 324 us
  waiting for transfers between devices  113 us (35%)
  blocking collectives  75.4 us (23%)
  Pallas kernels  48.7 us (15%)
  starting transfers between devices  33.5 us (10%)
  matrix products  18.7 us (6%)
  between operations  15.3 us (5%)
  local copies, waits for them, and re-layouts  10.1 us (3%)
  other arithmetic  9.53 us (3%)
    all_to_all x5, waiting for transfers between devices, exchange(): lax.all_to_all(block, EXPERT, split_axis=0, concat_axis=0, tiled=True)  80.5 us
    all_to_all x1, blocking collectives, exchange(): lax.all_to_all(block, EXPERT, split_axis=0, concat_axis=0, tiled=True)  50.3 us
    all_to_all x5, starting transfers between devices, exchange(): lax.all_to_all(block, EXPERT, split_axis=0, concat_axis=0, tiled=True)  27.2 us
    all_gather x1, waiting for transfers between devices, on_device(): cond_full = lax.all_gather(cond_part, DP, axis=0, tiled=True)  22.9 us
    dot_general x3, matrix products, matmul(): lax.dot_general(left, right, (((left_dim,), (right_dim,)), ((), ())), pre...  16 us
    all_gather x1, blocking collectives, on_device(): small = lax.all_gather(small, 'y', axis=0, tiled=True)  13.5 us
    all_gather x1, blocking collectives, on_device(): small = lax.all_gather(small, DP, axis=0, tiled=True)  11.6 us
    pallas_call x1, Pallas kernels, on_device(): call(cond_grad_kernel, (width // block,), [once(rows, features), once(row...  10.2 us
  transfers between devices with their start and end apart: 9, of which 8 were waited for; matrix products, arithmetic and copies ran while one was open for 6% of the time, Pallas kernels for 3%

profile of v1, /device:TPU:36, one launch (start us, length us, event | category | flops | bytes accessed | tf_op | source)
XLA Modules:
  0.0 324.4 jit_solution(8588977594851773107)
XLA Ops:
  7.3 8.5 %conditional.2 = (f32[4,128,768]{2,1,0:T(8,128)}, f32[4,16,128]{2,1,0:T(8,128)}) conditional(s32[]{:T(128)} %convert_element_type.36, () %tuple.25, (s32[4,128]{1,0:T(4,128)}, f32[16,128]{1,0:T(8,128)}, f32[4,16,128]{2,1,0:T(8,128)}, bf16[16,768]{1,0:T(8,128)(2,1)}) %tuple.26), branch_computations={%region_0.0_spmd, %region_1.0_spmd} | conditional | flops 76509056 | bytes 4869136 | solution.py:576
  15.8 4.4 %shard_map.172 = (bf16[32,112,256]{2,1,0:T(8,128)(2,1)}, bf16[32,72,512]{2,1,0:T(8,128)(2,1)}, f32[768,128]{1,0:T(8,128)}, f32[128,1]{1,0:T(8,128)}) custom-call(bf16[128,3072]{1,0:T(8,128)(2,1)S(1)} %copy-done.1, f32[1,3072]{1,0:T(1,128)S(1)} %bitcast.38, s32[4,128]{1,0:T(4,128)S(1)} %bitcast.41, f32[4,128]{1,0:T(4,128)S(1)} %bitcast.42, ...), custom_call_target="tpu_custom_call" | custom-call | flops 800000000 | bytes 5000000 | tf_op jit(solution)/shard_map/pallas_call | solution.py:538
  20.2 50.3 %all_to_all.35.rows_ref = bf16[32,112,256]{2,1,0:T(8,128)(2,1)S(1)} all-to-all(bf16[32,112,256]{2,1,0:T(8,128)(2,1)} %get-tuple-element.67), channel_id=1, replica_groups=mesh['x'=4,'core'=2,'y'=4,'z'=8] {'y','z'}, dimensions={0} | all-to-all | bytes 3670016 | tf_op jit(solution)/shard_map/all_to_all | solution.py:497
  72.1 5.1 %all-to-all-start = ((bf16[32,72,512]{2,1,0:T(8,128)(2,1)}), bf16[32,72,512]{2,1,0:T(8,128)(2,1)}, u32[]{:S(2)}, u32[]{:S(2)}) async-start(bf16[32,72,512]{2,1,0:T(8,128)(2,1)} %get-tuple-element.63), calls=%async_computation | async-start | bytes 4718592 | tf_op jit(solution)/shard_map/all_to_all | solution.py:497
  81.2 22.9 %all-gather.2.cloned.1.call-done = bf16[3072,768]{1,0:T(8,128)(2,1)} async-done(((bf16[384,768]{1,0:T(8,128)(2,1)}), bf16[3072,768]{1,0:T(8,128)(2,1)}) %all-gather.2.cloned.1.call-update) | async-done | bytes 4718608 | tf_op jit(solution)/shard_map/all_gather | solution.py:583
  104.1 8.7 %fusion.9.mixed_in = bf16[768,768]{1,0:T(8,128)(2,1)} fusion(bf16[3072,768]{1,0:T(8,128)(2,1)} %all-gather.2.cloned.1.call-done, bf16[1,768,3072]{2,1,0:T(8,128)(2,1)} %param.22), kind=kOutput, calls=%fused_computation.26 | convolution fusion | flops 3624468480 | bytes 10616832 | tf_op jit(solution)/shard_map/dot_general | solution.py:70
  112.8 13.8 %all-to-all-done.rows_ref = bf16[32,72,512]{2,1,0:T(8,128)(2,1)} async-done(((bf16[32,72,512]{2,1,0:T(8,128)(2,1)}), bf16[32,72,512]{2,1,0:T(8,128)(2,1)}, u32[]{:S(2)}, u32[]{:S(2)}) %all-to-all-start) | async-done | bytes 2359328 | tf_op jit(solution)/shard_map/all_to_all | solution.py:497
  127.8 9.0 %shard_map.174 = (f32[576,768]{1,0:T(8,128)}, bf16[576,768]{1,0:T(8,128)(2,1)}, bf16[32,56,256]{2,1,0:T(8,128)(2,1)}) custom-call(bf16[32,72,512]{2,1,0:T(8,128)(2,1)} %all-to-all-done.rows_ref, bf16[3072,768]{1,0:T(8,128)(2,1)} %bitcast.35, f32[576,768]{1,0:T(8,128)S(1)} %copy-done.4, bf16[768,768]{1,0:T(8,128)(2,1)S(1)} %copy-done.18), custom_call_target="tpu_custom_call" | custom-call | flops 2717908992 | bytes 10000000 | tf_op jit(solution)/shard_map/pallas_call | solution.py:598
  136.9 6.0 %all-to-all-start.2 = ((bf16[32,56,256]{2,1,0:T(8,128)(2,1)}), bf16[32,56,256]{2,1,0:T(8,128)(2,1)S(1)}, u32[]{:S(2)}, u32[]{:S(2)}) async-start(bf16[32,56,256]{2,1,0:T(8,128)(2,1)} %get-tuple-element.68), calls=%async_computation.2 | async-start | bytes 1835008 | tf_op jit(solution)/shard_map/all_to_all | solution.py:497
  146.4 15.1 %all-to-all-done.2.added_ref = bf16[32,56,256]{2,1,0:T(8,128)(2,1)S(1)} async-done(((bf16[32,56,256]{2,1,0:T(8,128)(2,1)}), bf16[32,56,256]{2,1,0:T(8,128)(2,1)S(1)}, u32[]{:S(2)}, u32[]{:S(2)}) %all-to-all-start.2) | async-done | bytes 917536 | tf_op jit(solution)/shard_map/all_to_all | solution.py:497
  161.6 6.2 %shard_map.175 = (bf16[128,768]{1,0:T(8,128)(2,1)}, bf16[32,64,256]{2,1,0:T(8,128)(2,1)}) custom-call(bf16[32,56,256]{2,1,0:T(8,128)(2,1)S(1)} %all-to-all-done.2.added_ref, f32[128,768]{1,0:T(8,128)S(1)} %convolution_bitcast_fusion.direct_ref, f32[4,128,768]{2,1,0:T(8,128)} %get-tuple-element.71.offset_in, f32[4,16,128]{2,1,0:T(8,128)} %get-tuple-element.72.noisy_ref, ...), custom_call_target="tpu_custom_call" | custom-call | flops 1500000000 | bytes 5000000 | tf_op jit(solution)/shard_map/pallas_call | solution.py:622
  167.7 5.3 %all-to-all-start.3 = ((bf16[32,64,256]{2,1,0:T(8,128)(2,1)}), bf16[32,64,256]{2,1,0:T(8,128)(2,1)}, u32[]{:S(2)}, u32[]{:S(2)}) async-start(bf16[32,64,256]{2,1,0:T(8,128)(2,1)} %get-tuple-element.74), calls=%async_computation.3 | async-start | bytes 2097152 | tf_op jit(solution)/shard_map/all_to_all | solution.py:497
  175.6 18.5 %all-to-all-done.3.grads_ref = bf16[32,64,256]{2,1,0:T(8,128)(2,1)} async-done(((bf16[32,64,256]{2,1,0:T(8,128)(2,1)}), bf16[32,64,256]{2,1,0:T(8,128)(2,1)}, u32[]{:S(2)}, u32[]{:S(2)}) %all-to-all-start.3) | async-done | bytes 1048608 | tf_op jit(solution)/shard_map/all_to_all | solution.py:497
  195.4 7.6 %shard_map.176 = (bf16[576,768]{1,0:T(8,128)(2,1)}, bf16[576,768]{1,0:T(8,128)(2,1)}, f32[8,128]{1,0:T(8,128)}, bf16[32,72,384]{2,1,0:T(8,128)(2,1)}) custom-call(bf16[32,64,256]{2,1,0:T(8,128)(2,1)} %all-to-all-done.3.grads_ref, bf16[768,768]{1,0:T(8,128)(2,1)S(1)} %copy-done.19, f32[576,768]{1,0:T(8,128)S(1)} %fusion.8.slope_ref, bf16[3072,768]{1,0:T(8,128)(2,1)} %bitcast.36), custom_call_target="tpu_custom_call" | custom-call | flops 2717908992 | bytes 10000000 | tf_op jit(solution)/shard_map/pallas_call | solution.py:652
  204.2 10.2 %shard_map.180 = bf16[3072,768]{1,0:T(8,128)(2,1)} custom-call(bf16[576,768]{1,0:T(8,128)(2,1)S(1)} %copy-done.5, bf16[576,768]{1,0:T(8,128)(2,1)S(1)} %copy-done.6, bf16[768,3072]{1,0:T(8,128)(2,1)} %bitcast.44, bf16[128,3072]{1,0:T(8,128)(2,1)S(1)} %copy-done.1, bf16[128,768]{1,0:T(8,128)(2,1)S(1)} %copy-done.8), custom_call_target="tpu_custom_call" | custom-call | tf_op jit(solution)/shard_map/pallas_call | solution.py:692
  214.5 5.3 %all-to-all-start.5 = ((bf16[32,72,384]{2,1,0:T(8,128)(2,1)}), bf16[32,72,384]{2,1,0:T(8,128)(2,1)S(1)}, u32[]{:S(2)}, u32[]{:S(2)}) async-start(bf16[32,72,384]{2,1,0:T(8,128)(2,1)} %get-tuple-element.78), calls=%async_computation.5 | async-start | bytes 3538944 | tf_op jit(solution)/shard_map/all_to_all | solution.py:497
  222.1 4.0 %shard_map.177 = bf16[32,72,384]{2,1,0:T(8,128)(2,1)} custom-call(bf16[576,768]{1,0:T(8,128)(2,1)S(1)} %copy-done.7, bf16[3072,768]{1,0:T(8,128)(2,1)S(1)} %bitcast.37), custom_call_target="tpu_custom_call" | custom-call | tf_op jit(solution)/shard_map/pallas_call | solution.py:678
  226.1 29.8 %all-to-all-done.5.block_ref = bf16[32,72,384]{2,1,0:T(8,128)(2,1)S(1)} async-done(((bf16[32,72,384]{2,1,0:T(8,128)(2,1)}), bf16[32,72,384]{2,1,0:T(8,128)(2,1)S(1)}, u32[]{:S(2)}, u32[]{:S(2)}) %all-to-all-start.5) | async-done | bytes 1769504 | tf_op jit(solution)/shard_map/all_to_all | solution.py:497
  257.1 5.4 %all-to-all-start.4 = ((bf16[32,72,384]{2,1,0:T(8,128)(2,1)}), bf16[32,72,384]{2,1,0:T(8,128)(2,1)S(1)}, u32[]{:S(2)}, u32[]{:S(2)}) async-start(bf16[32,72,384]{2,1,0:T(8,128)(2,1)} %shard_map.177), calls=%async_computation.4 | async-start | bytes 3538944 | tf_op jit(solution)/shard_map/all_to_all | solution.py:497
  263.3 11.6 %all_gather.10 = f32[64,128]{1,0:T(8,128)S(1)} all-gather(f32[8,128]{1,0:T(8,128)S(1)} %copy-done.24), channel_id=1, replica_groups=mesh['x'=4,'core'=2,'y'=4,'z'=8] {'x','core'}, dimensions={0}, use_global_device_ids=true | all-gather | bytes 36864 | tf_op jit(solution)/shard_map/all_gather | solution.py:711
  274.9 13.5 %all_gather.11 = bf16[64,128]{1,0:T(8,128)(2,1)S(1)} all-gather(bf16[16,128]{1,0:T(8,128)(2,1)S(1)} %pad_maximum_fusion.1), channel_id=1, replica_groups=mesh['x'=4,'core'=2,'y'=4,'z'=8] {'y'}, dimensions={0}, use_global_device_ids=true | all-gather | bytes 20480 | tf_op jit(solution)/shard_map/all_gather | solution.py:715
  288.4 5.1 %reduce-scatter.5.cloned.1.call-done = bf16[96,768]{1,0:T(8,128)(2,1)} async-done(((bf16[384,768]{1,0:T(8,128)(2,1)}), bf16[96,768]{1,0:T(8,128)(2,1)}) %reduce-scatter.5.cloned.1.call-update) | async-done | bytes 147472 | tf_op jit(solution)/shard_map/reduce_scatter | solution.py:709
  298.7 6.2 %all-to-all-start.6 = ((bf16[8,136,128]{2,1,0:T(8,128)(2,1)}), bf16[8,136,128]{2,1,0:T(8,128)(2,1)S(1)}, u32[]{:S(2)}, u32[]{:S(2)}) async-start(bf16[8,136,128]{2,1,0:T(8,128)(2,1)} %pad_maximum_fusion), calls=%async_computation.8 | async-start | bytes 557056 | tf_op jit(solution)/shard_map/all_to_all | solution.py:751
  304.8 4.1 %fusion.12.layer_ref = f32[128,3072]{1,0:T(8,128)S(1)} fusion(bf16[128,768]{1,0:T(8,128)(2,1)S(1)} %copy-done.9, bf16[3072,768]{1,0:T(8,128)(2,1)} %all-gather.2.cloned.1.call-done), kind=kOutput, calls=%fused_computation.35 | convolution fusion | flops 603979776 | bytes 6488064 | tf_op jit(solution)/shard_map/dot_general | solution.py:70
  (86 shorter events, 41.0 us)
Async XLA Ops:
  7.2 97.0 %all-gather.2.cloned.1.call-start = ((), (), s32[]{:S(2)}) async-start(), calls=%async_computation.9 | async-start | bytes 5308416 | tf_op jit(solution)/shard_map/all_gather | solution.py:583
  7.2 8.6 %copy-start.1 = (bf16[128,3072]{1,0:T(8,128)(2,1)S(1)}, bf16[128,3072]{1,0:T(8,128)(2,1)}, u32[]{:S(2)}) copy-start(bf16[128,3072]{1,0:T(8,128)(2,1)} %tokens_ref.5) | copy-start | bytes 2359300
  7.2 8.5 %copy-start.13 = (f32[3072]{0:T(1024)S(1)}, f32[3072]{0:T(1024)}, u32[]{:S(2)}) copy-start(f32[3072]{0:T(1024)} %param.18) | copy-start | bytes 36868
  7.2 8.5 %copy-start.14 = (bf16[12,768]{1,0:T(8,128)(2,1)S(1)}, bf16[12,768]{1,0:T(8,128)(2,1)}, u32[]{:S(2)}) copy-start(bf16[12,768]{1,0:T(8,128)(2,1)} %cond_in.1) | copy-start | bytes 55300
  7.2 8.5 %copy-start.16 = (s32[128,4]{0,1:T(4,128)S(1)}, s32[128,4]{0,1:T(4,128)}, u32[]{:S(2)}) copy-start(s32[128,4]{0,1:T(4,128)} %param.19) | copy-start | bytes 6148
  7.3 8.5 %copy-start.17 = (f32[128,4]{0,1:T(4,128)S(1)}, f32[128,4]{0,1:T(4,128)}, u32[]{:S(2)}) copy-start(f32[128,4]{0,1:T(4,128)} %param.20) | copy-start | bytes 6148
  72.1 54.4 %all-to-all-start = ((bf16[32,72,512]{2,1,0:T(8,128)(2,1)}), bf16[32,72,512]{2,1,0:T(8,128)(2,1)}, u32[]{:S(2)}, u32[]{:S(2)}) async-start(bf16[32,72,512]{2,1,0:T(8,128)(2,1)} %get-tuple-element.63), calls=%async_computation | async-start | bytes 4718592 | tf_op jit(solution)/shard_map/all_to_all | solution.py:497
  81.2 45.4 %copy-start.4 = (f32[576,768]{1,0:T(8,128)S(1)}, f32[576,768]{1,0:T(8,128)}, u32[]{:S(2)}) copy-start(f32[576,768]{1,0:T(8,128)} %shard_map.173.start_in) | copy-start | bytes 5308420
  136.8 6.1 %copy-start.20 = (f32[4,16,128]{2,1,0:T(8,128)S(1)}, f32[4,16,128]{2,1,0:T(8,128)}, u32[]{:S(2)}) copy-start(f32[4,16,128]{2,1,0:T(8,128)} %noise_in.1) | copy-start | bytes 98308
  136.8 6.1 %copy-start.21 = (bf16[16,768]{1,0:T(8,128)(2,1)S(1)}, bf16[16,768]{1,0:T(8,128)(2,1)}, u32[]{:S(2)}) copy-start(bf16[16,768]{1,0:T(8,128)(2,1)} %param.24) | copy-start | bytes 73732
  136.8 6.1 %copy-start.22 = (f32[16,128]{1,0:T(8,128)S(1)}, f32[16,128]{1,0:T(8,128)}, u32[]{:S(2)}) copy-start(f32[16,128]{1,0:T(8,128)} %param.27) | copy-start | bytes 24580
  136.9 24.7 %all-to-all-start.2 = ((bf16[32,56,256]{2,1,0:T(8,128)(2,1)}), bf16[32,56,256]{2,1,0:T(8,128)(2,1)S(1)}, u32[]{:S(2)}, u32[]{:S(2)}) async-start(bf16[32,56,256]{2,1,0:T(8,128)(2,1)} %get-tuple-element.68), calls=%async_computation.2 | async-start | bytes 1835008 | tf_op jit(solution)/shard_map/all_to_all | solution.py:497
  143.2 18.3 %copy-start.10 = (f32[768,128]{1,0:T(8,128)S(1)}, f32[768,128]{1,0:T(8,128)}, u32[]{:S(2)}) copy-start(f32[768,128]{1,0:T(8,128)} %get-tuple-element.73.gate_in.gate_ref) | copy-start | bytes 1179652
  143.2 18.3 %copy-start.15 = (bf16[16,768]{1,0:T(8,128)(2,1)S(1)}, bf16[16,768]{1,0:T(8,128)(2,1)}, u32[]{:S(2)}) copy-start(bf16[16,768]{1,0:T(8,128)(2,1)} %out_in.1) | copy-start | bytes 73732
  167.7 26.4 %all-to-all-start.3 = ((bf16[32,64,256]{2,1,0:T(8,128)(2,1)}), bf16[32,64,256]{2,1,0:T(8,128)(2,1)}, u32[]{:S(2)}, u32[]{:S(2)}) async-start(bf16[32,64,256]{2,1,0:T(8,128)(2,1)} %get-tuple-element.74), calls=%async_computation.3 | async-start | bytes 2097152 | tf_op jit(solution)/shard_map/all_to_all | solution.py:497
  173.0 89.6 %reduce-scatter.3.cloned.1.call-start = ((), (), s32[]{:S(2)}) async-start(), calls=%async_computation.10 | async-start | bytes 5308416 | tf_op jit(solution)/shard_map/reduce_scatter | solution.py:708
  175.6 27.4 %copy-start.5 = (bf16[576,768]{1,0:T(8,128)(2,1)S(1)}, bf16[576,768]{1,0:T(8,128)(2,1)}, u32[]{:S(2)}) copy-start(bf16[576,768]{1,0:T(8,128)(2,1)} %get-tuple-element.84.hidden_ref) | copy-start | bytes 2654212
  195.4 7.7 %copy-start.8 = (bf16[128,768]{1,0:T(8,128)(2,1)S(1)}, bf16[128,768]{1,0:T(8,128)(2,1)}, u32[]{:S(2)}) copy-start(bf16[128,768]{1,0:T(8,128)(2,1)} %get-tuple-element.82.delta_ref) | copy-start | bytes 589828
  214.5 41.5 %all-to-all-start.5 = ((bf16[32,72,384]{2,1,0:T(8,128)(2,1)}), bf16[32,72,384]{2,1,0:T(8,128)(2,1)S(1)}, u32[]{:S(2)}, u32[]{:S(2)}) async-start(bf16[32,72,384]{2,1,0:T(8,128)(2,1)} %get-tuple-element.78), calls=%async_computation.5 | async-start | bytes 3538944 | tf_op jit(solution)/shard_map/all_to_all | solution.py:497
  226.1 37.1 %copy-start.24 = (f32[8,128]{1,0:T(8,128)S(1)}, f32[8,128]{1,0:T(8,128)}, u32[]{:S(2)}) copy-start(f32[8,128]{1,0:T(8,128)} %get-tuple-element.86) | copy-start | bytes 12292
  257.1 41.5 %all-to-all-start.4 = ((bf16[32,72,384]{2,1,0:T(8,128)(2,1)}), bf16[32,72,384]{2,1,0:T(8,128)(2,1)S(1)}, u32[]{:S(2)}, u32[]{:S(2)}) async-start(bf16[32,72,384]{2,1,0:T(8,128)(2,1)} %shard_map.177), calls=%async_computation.4 | async-start | bytes 3538944 | tf_op jit(solution)/shard_map/all_to_all | solution.py:497
  262.5 42.3 %copy-start.9 = (bf16[128,768]{1,0:T(8,128)(2,1)S(1)}, bf16[128,768]{1,0:T(8,128)(2,1)}, u32[]{:S(2)}) copy-start(bf16[128,768]{1,0:T(8,128)(2,1)} %get-tuple-element.82.delta_ref) | copy-start | bytes 589828
  262.6 31.0 %reduce-scatter.5.cloned.1.call-start = ((), (), s32[]{:S(2)}) async-start(), calls=%async_computation.11 | async-start | bytes 737280 | tf_op jit(solution)/shard_map/reduce_scatter | solution.py:709
  298.7 16.8 %all-to-all-start.6 = ((bf16[8,136,128]{2,1,0:T(8,128)(2,1)}), bf16[8,136,128]{2,1,0:T(8,128)(2,1)S(1)}, u32[]{:S(2)}, u32[]{:S(2)}) async-start(bf16[8,136,128]{2,1,0:T(8,128)(2,1)} %pad_maximum_fusion), calls=%async_computation.8 | async-start | bytes 557056 | tf_op jit(solution)/shard_map/all_to_all | solution.py:751
  (11 other events, 33.9 us)
Sparse Core Ops, SparseCore 0:
  72.2 31.8 all-gather.1
  214.6 33.3 reduce-scatter.2
  265.9 27.5 reduce-scatter.4
